TPU v7x, 256 devices: a whole 4x4x8 slice. The times are simulated.
256 devices in a mesh: pair: 8 (over x, core), node: 32 (over z, y).
Axes of the slice: x: 4, y: 4, z: 8, core: 2. Of those that a mesh axis runs over, the one named last changes fastest.
Arguments:
- features: bfloat16 [32768, 256], P('node', 'pair'), may hold values from -60 to 60
- neighbors: int32 [8, 32768, 10], P('pair', 'node'), may hold values from 0 to 32767, as said below
- counts: int32 [8, 32768], P('pair', 'node'), may hold values from 1 to 10
- pairs: int32 [1048576, 2], P(('pair', 'node')), may hold values from 0 to 32767, as said below
- w_self: bfloat16 [256, 256], replicated, may hold values from -0.25 to 0.25
- w_neigh: bfloat16 [256, 256], replicated, may hold values from -0.25 to 0.25
- b_layer: float32 [256], replicated, may hold values from -3 to 3
- w_one: bfloat16 [256, 256], replicated, may hold values from -0.375 to 0.375
- b_one: float32 [256], replicated, may hold values from -3 to 3
- w_two: bfloat16 [256, 256], replicated, may hold values from -0.375 to 0.375
- b_two: float32 [256], replicated, may hold values from -3 to 3
- w_out: float32 [256], replicated, may hold values from -0.375 to 0.375
Outputs:
- pair_loss: float32 [1048576], P(('pair', 'node'))
Inputs may be any that keep to these rules, and one draw needn't show every extreme that they name: `neighbors`: within one list block (one micro-batch, the 1024 nodes of one node range) at most 640 slots name nodes of any one node range; in every micro-batch one node range receives exactly 640 from every block. `pairs`: within the 4096 rows of one device at most 512 endpoints lie in any one node range; in every micro-batch one node range receives exactly 512 from every device.
All inputs are finite; a program needn't handle non-finite values.
Results may differ from a plain program's by a relative error of at most 0.0032.
Values may be sent and summed in bfloat16 or wider, within the bound.
No kernel may reach another device: no remote copies, remote signals or barrier semaphores. Data moves between devices by JAX's collectives and lax.ppermute only.
A program may use at most 128 MiB of HBM per device.

v0:
```python
import jax
import jax.numpy as jnp
from jax import lax
from jax.sharding import PartitionSpec as P


def bucket(ids, shards, per_shard):
    owner = ids // per_shard
    offset = ids - owner * per_shard
    capacity = 2 * ids.shape[0] // shards
    hits = (owner[:, None] == jnp.arange(shards, dtype=jnp.int32)[None, :]).astype(jnp.int32)
    slot = jnp.sum(jnp.cumsum(hits, axis=0) * hits, axis=1) - 1
    target = owner * capacity + slot
    requests = jnp.zeros((shards * capacity,), jnp.int32).at[target].set(offset)
    return (requests.reshape(shards, capacity), target)


def slot_sums(targets, valid, source):
    nodes = targets.shape[0]
    fanout = targets.shape[1]
    span = source.shape[0]
    block = min(128, nodes)
    columns = jnp.arange(span, dtype=jnp.int32)
    slot_mask = jnp.arange(fanout, dtype=jnp.int32)[None, :] < valid[:, None]
    marked = jnp.where(slot_mask, targets, -1)

    def one_block(block_targets):
        tallies = jnp.zeros((block, span), jnp.bfloat16)
        for slot in range(fanout):
            tallies = tallies + (block_targets[:, slot][:, None] == columns[None, :]).astype(
                jnp.bfloat16
            )
        return jnp.dot(tallies, source, preferred_element_type=jnp.float32)

    summed = lax.map(one_block, marked.reshape(nodes // block, block, fanout))
    return summed.reshape(nodes, source.shape[1])


def layer_rows(self_rows, summed, valid, w_self, w_neigh, b_layer):
    mean_nbr = (summed / valid[:, None].astype(jnp.float32)).astype(jnp.bfloat16)
    pre = jnp.dot(self_rows, w_self, preferred_element_type=jnp.float32)
    pre = pre + jnp.dot(mean_nbr, w_neigh, preferred_element_type=jnp.float32) + b_layer
    active = jnp.maximum(pre, 0.0)
    return (active * lax.rsqrt(jnp.mean(active * active, axis=-1, keepdims=True) + 1e-06)).astype(
        jnp.bfloat16
    )


def on_device(
    features, neighbors, counts, pairs, w_self, w_neigh, b_layer, w_one, b_one, w_two, b_two, w_out
):
    shards = lax.axis_size("node")
    table = lax.all_gather(features, "pair", axis=1, tiled=True)
    per_shard = table.shape[0]
    width = table.shape[1]
    fanout = neighbors.shape[2]
    nbr_flat = neighbors.reshape(-1)
    end_flat = pairs.reshape(-1)
    requests, target = bucket(nbr_flat, shards, per_shard)
    replies = lax.all_to_all(
        jnp.take(
            table, lax.all_to_all(requests, "node", split_axis=0, concat_axis=0, tiled=True), axis=0
        ),
        "node",
        split_axis=0,
        concat_axis=0,
        tiled=True,
    )
    summed = slot_sums(target.reshape(per_shard, fanout), counts[0], replies.reshape(-1, width))
    embed = layer_rows(table, summed, counts[0], w_self, w_neigh, b_layer)
    end_requests, end_target = bucket(end_flat, shards, per_shard)
    end_replies = lax.all_to_all(
        jnp.take(
            embed,
            lax.all_to_all(end_requests, "node", split_axis=0, concat_axis=0, tiled=True),
            axis=0,
        ),
        "node",
        split_axis=0,
        concat_axis=0,
        tiled=True,
    )
    ends = jnp.take(end_replies.reshape(-1, width), end_target, axis=0)
    ends = ends.reshape(pairs.shape[0], 2, width)
    hadamard = (ends[:, 0, :].astype(jnp.float32) * ends[:, 1, :].astype(jnp.float32)).astype(
        jnp.bfloat16
    )
    first = jnp.maximum(
        jnp.dot(hadamard, w_one, preferred_element_type=jnp.float32) + b_one, 0.0
    ).astype(jnp.bfloat16)
    second = jnp.maximum(jnp.dot(first, w_two, preferred_element_type=jnp.float32) + b_two, 0.0)
    logit = jnp.dot(second, w_out, precision=lax.Precision.HIGHEST)
    local_pairs = pairs.shape[0]
    positive = jnp.arange(local_pairs, dtype=jnp.int32) < local_pairs // 4
    return jnp.where(positive, jax.nn.softplus(-logit), jax.nn.softplus(logit))


def solution(mesh):
    in_specs = (
        P("node", "pair"),
        P("pair", "node", None),
        P("pair", "node"),
        P(("pair", "node"), None),
        P(),
        P(),
        P(),
        P(),
        P(),
        P(),
        P(),
        P(),
    )
    out_specs = P(("pair", "node"))
    return jax.shard_map(
        on_device, mesh=mesh, in_specs=in_specs, out_specs=out_specs, check_vma=False
    )
```

profile of v0, /device:TPU:1, one launch (start us, length us, event | category | flops | bytes accessed | tf_op | source)
XLA Modules:
  0.0 967.2 jit_solution(6802900664072725730)
XLA Ops:
  2.3 9.7 %reduce-window.16 = s32[32,80,128]{2,1,0:T(8,128)S(1)} reduce-window(s32[32,80,128]{2,1,0:T(8,128)S(1)} %fusion.64, s32[]{:T(128)} %copy.91), window={size=1x1x128 pad=0_0x0_0x127_0}, to_apply=%region_4.5 | reduce-window | flops 41615360 | bytes 2621444 | tf_op jit(solution)/shard_map/reduce-window.2
  14.6 38.5 %scatter_custom_fusion.1 = s32[20480]{0:T(1024)} fusion(s32[10240]{0:T(1024)S(1)} %bitcast.124, s32[10240]{0:T(1024)S(1)} %get-tuple-element.122, s32[]{:T(128)} %copy.91), kind=kCustom, calls=%fused_computation.149 | custom fusion | bytes 81924 | tf_op jit(solution)/shard_map/scatter | solution.py:14
  53.1 12.0 %all-to-all-start.1 = ((s32[32,1,640]{2,1,0:T(1,128)}), s32[32,1,640]{2,1,0:T(1,128)S(1)}, u32[]{:S(2)}, u32[]{:S(2)}) async-start(s32[32,1,640]{2,1,0:T(1,128)} %bitcast.9), calls=%async_computation.1 | async-start | bytes 163840 | tf_op jit(solution)/shard_map/all_to_all | solution.py:62
  69.8 9.5 reduce-window.14
  82.3 27.0 %all_gather.3 = bf16[1024,256]{0,1:T(8,128)(2,1)S(1)} all-gather(bf16[1024,32]{0,1:T(8,128)(2,1)S(1)} %copy-done.10), channel_id=1, replica_groups=mesh['pair'=8,'node'=32] {'pair'}, dimensions={1}, use_global_device_ids=true | all-gather | bytes 589824 | tf_op jit(solution)/shard_map/all_gather | solution.py:53
  109.5 31.1 %scatter_custom_fusion = s32[16384]{0:T(1024)} fusion(s32[8192]{0:T(1024)S(1)} %bitcast.119, s32[8192]{0:T(1024)S(1)} %get-tuple-element.124, s32[]{:T(128)} %copy.91), kind=kCustom, calls=%fused_computation.162 | custom fusion | bytes 65540 | tf_op jit(solution)/shard_map/scatter | solution.py:14
  140.5 9.5 all-to-all-start
  150.1 80.8 %gather_fusion = bf16[20480,256]{1,0:T(8,128)(2,1)} fusion(bf16[1024,256]{1,0:T(8,128)(2,1)S(1)} %copy.62, s32[20480]{0:T(1024)S(1)} %broadcast_clamp_fusion), kind=kCustom, calls=%fused_computation | custom fusion | bytes 21053440 | tf_op jit(solution)/shard_map/jit(_take)/gather | solution.py:61
  230.9 9.7 %broadcast_select_fusion = bf16[32,640,256]{2,1,0:T(8,128)(2,1)} fusion(bf16[32,640,256]{2,1,0:T(8,128)(2,1)} %bitcast.109, pred[32,640]{1,0:T(8,128)(4,1)S(1)} %compare_and_fusion), kind=kLoop, calls=%fused_computation.60 | loop fusion | flops 5242880 | bytes 20992000 | tf_op jit(solution)/shard_map/jit(_take)/select_n | solution.py:61
  240.7 9.5 all-to-all-start.2
  251.4 232.0 %all-to-all-done.2 = bf16[32,640,256]{2,1,0:T(8,128)(2,1)} async-done(((bf16[32,640,256]{2,1,0:T(8,128)(2,1)}), bf16[32,640,256]{2,1,0:T(8,128)(2,1)}, u32[]{:S(2)}, u32[]{:S(2)}) %all-to-all-start.2) | async-done | bytes 10485792 | tf_op jit(solution)/shard_map/all_to_all | solution.py:60
  483.4 139.1 %while.12 = (s32[]{:T(128)}, f32[8,128,256]{2,1,0:T(8,128)S(1)}, s32[8,128,10]{1,0,2:T(8,128)S(1)}, bf16[20480,256]{1,0:T(8,128)(2,1)}, s32[]{:T(128)}) while((s32[]{:T(128)}, f32[8,128,256]{2,1,0:T(8,128)S(1)}, s32[8,128,10]{1,0,2:T(8,128)S(1)}, bf16[20480,256]{1,0:T(8,128)(2,1)}, s32[]{:T(128)}) %tuple.41), condition=%wide.region_9.10_spmd.clone.clone, body=%wide.region_8.9_spmd.clone.clone.sunk | while | flops 1447034880 | bytes 10652741 | solution.py:35
  483.5 17.3 %fusion.104 = f32[8,128,256]{2,1,0:T(8,128)S(1)} fusion(f32[8,128,256]{2,1,0:T(8,128)S(1)} %get-tuple-element.179, s32[]{:T(128)} %get-tuple-element.178, bf16[20480,256]{1,0:T(8,128)(2,1)} %get-tuple-element.186, s32[128]{0:T(128)S(1)} %get-tuple-element.163, s32[128]{0:T(128)S(1)} %get-tuple-element.164, s32[128]{0:T(128)S(1)} %get-tuple-element.165, ...), kind=kOutput, calls=%fused_computation.47.clone.1 | convolution fusion | flops 1447034880 | bytes 10621956 | tf_op jit(solution)/shard_map/while/body/eval_jaxpr/dot_general | solution.py:33
  500.8 17.3 %fusion.104 = f32[8,128,256]{2,1,0:T(8,128)S(1)} fusion(f32[8,128,256]{2,1,0:T(8,128)S(1)} %get-tuple-element.179, s32[]{:T(128)} %get-tuple-element.178, bf16[20480,256]{1,0:T(8,128)(2,1)} %get-tuple-element.186, s32[128]{0:T(128)S(1)} %get-tuple-element.163, s32[128]{0:T(128)S(1)} %get-tuple-element.164, s32[128]{0:T(128)S(1)} %get-tuple-element.165, ...), kind=kOutput, calls=%fused_computation.47.clone.1 | convolution fusion | flops 1447034880 | bytes 10621956 | tf_op jit(solution)/shard_map/while/body/eval_jaxpr/dot_general | solution.py:33
  518.2 17.3 %fusion.104 = f32[8,128,256]{2,1,0:T(8,128)S(1)} fusion(f32[8,128,256]{2,1,0:T(8,128)S(1)} %get-tuple-element.179, s32[]{:T(128)} %get-tuple-element.178, bf16[20480,256]{1,0:T(8,128)(2,1)} %get-tuple-element.186, s32[128]{0:T(128)S(1)} %get-tuple-element.163, s32[128]{0:T(128)S(1)} %get-tuple-element.164, s32[128]{0:T(128)S(1)} %get-tuple-element.165, ...), kind=kOutput, calls=%fused_computation.47.clone.1 | convolution fusion | flops 1447034880 | bytes 10621956 | tf_op jit(solution)/shard_map/while/body/eval_jaxpr/dot_general | solution.py:33
  535.6 17.3 %fusion.104 = f32[8,128,256]{2,1,0:T(8,128)S(1)} fusion(f32[8,128,256]{2,1,0:T(8,128)S(1)} %get-tuple-element.179, s32[]{:T(128)} %get-tuple-element.178, bf16[20480,256]{1,0:T(8,128)(2,1)} %get-tuple-element.186, s32[128]{0:T(128)S(1)} %get-tuple-element.163, s32[128]{0:T(128)S(1)} %get-tuple-element.164, s32[128]{0:T(128)S(1)} %get-tuple-element.165, ...), kind=kOutput, calls=%fused_computation.47.clone.1 | convolution fusion | flops 1447034880 | bytes 10621956 | tf_op jit(solution)/shard_map/while/body/eval_jaxpr/dot_general | solution.py:33
  552.9 17.3 %fusion.104 = f32[8,128,256]{2,1,0:T(8,128)S(1)} fusion(f32[8,128,256]{2,1,0:T(8,128)S(1)} %get-tuple-element.179, s32[]{:T(128)} %get-tuple-element.178, bf16[20480,256]{1,0:T(8,128)(2,1)} %get-tuple-element.186, s32[128]{0:T(128)S(1)} %get-tuple-element.163, s32[128]{0:T(128)S(1)} %get-tuple-element.164, s32[128]{0:T(128)S(1)} %get-tuple-element.165, ...), kind=kOutput, calls=%fused_computation.47.clone.1 | convolution fusion | flops 1447034880 | bytes 10621956 | tf_op jit(solution)/shard_map/while/body/eval_jaxpr/dot_general | solution.py:33
  570.3 17.3 %fusion.104 = f32[8,128,256]{2,1,0:T(8,128)S(1)} fusion(f32[8,128,256]{2,1,0:T(8,128)S(1)} %get-tuple-element.179, s32[]{:T(128)} %get-tuple-element.178, bf16[20480,256]{1,0:T(8,128)(2,1)} %get-tuple-element.186, s32[128]{0:T(128)S(1)} %get-tuple-element.163, s32[128]{0:T(128)S(1)} %get-tuple-element.164, s32[128]{0:T(128)S(1)} %get-tuple-element.165, ...), kind=kOutput, calls=%fused_computation.47.clone.1 | convolution fusion | flops 1447034880 | bytes 10621956 | tf_op jit(solution)/shard_map/while/body/eval_jaxpr/dot_general | solution.py:33
  587.6 17.3 %fusion.104 = f32[8,128,256]{2,1,0:T(8,128)S(1)} fusion(f32[8,128,256]{2,1,0:T(8,128)S(1)} %get-tuple-element.179, s32[]{:T(128)} %get-tuple-element.178, bf16[20480,256]{1,0:T(8,128)(2,1)} %get-tuple-element.186, s32[128]{0:T(128)S(1)} %get-tuple-element.163, s32[128]{0:T(128)S(1)} %get-tuple-element.164, s32[128]{0:T(128)S(1)} %get-tuple-element.165, ...), kind=kOutput, calls=%fused_computation.47.clone.1 | convolution fusion | flops 1447034880 | bytes 10621956 | tf_op jit(solution)/shard_map/while/body/eval_jaxpr/dot_general | solution.py:33
  605.0 17.3 %fusion.104 = f32[8,128,256]{2,1,0:T(8,128)S(1)} fusion(f32[8,128,256]{2,1,0:T(8,128)S(1)} %get-tuple-element.179, s32[]{:T(128)} %get-tuple-element.178, bf16[20480,256]{1,0:T(8,128)(2,1)} %get-tuple-element.186, s32[128]{0:T(128)S(1)} %get-tuple-element.163, s32[128]{0:T(128)S(1)} %get-tuple-element.164, s32[128]{0:T(128)S(1)} %get-tuple-element.165, ...), kind=kOutput, calls=%fused_computation.47.clone.1 | convolution fusion | flops 1447034880 | bytes 10621956 | tf_op jit(solution)/shard_map/while/body/eval_jaxpr/dot_general | solution.py:33
  623.5 64.8 %gather_fusion.1 = bf16[16384,256]{1,0:T(8,128)(2,1)} fusion(bf16[1024,256]{1,0:T(8,128)(2,1)S(1)} %copy.64, s32[16384]{0:T(1024)S(1)} %broadcast_clamp_fusion.1), kind=kCustom, calls=%fused_computation.1 | custom fusion | bytes 16842752 | tf_op jit(solution)/shard_map/jit(_take)/gather | solution.py:73
  696.3 19.9 %all-to-all-start.3 = ((bf16[32,512,256]{2,1,0:T(8,128)(2,1)}), bf16[32,512,256]{2,1,0:T(8,128)(2,1)}, u32[]{:S(2)}, u32[]{:S(2)}) async-start(bf16[32,512,256]{2,1,0:T(8,128)(2,1)} %broadcast_select_fusion.1), calls=%async_computation.3 | async-start | bytes 16777216 | tf_op jit(solution)/shard_map/all_to_all | solution.py:72
  719.2 187.4 %all-to-all-done.3 = bf16[32,512,256]{2,1,0:T(8,128)(2,1)} async-done(((bf16[32,512,256]{2,1,0:T(8,128)(2,1)}), bf16[32,512,256]{2,1,0:T(8,128)(2,1)}, u32[]{:S(2)}, u32[]{:S(2)}) %all-to-all-start.3) | async-done | bytes 8388640 | tf_op jit(solution)/shard_map/all_to_all | solution.py:72
  906.6 35.4 %gather_fusion.2 = bf16[8192,256]{1,0:T(8,128)(2,1)} fusion(bf16[16384,256]{1,0:T(8,128)(2,1)} %bitcast.19, s32[8192]{0:T(1024)S(1)} %broadcast_clamp_fusion.2), kind=kCustom, calls=%fused_computation.2 | custom fusion | bytes 8421376 | tf_op jit(solution)/shard_map/jit(_take)/gather | solution.py:83
  (114 shorter events, 50.7 us)
Async XLA Ops:
  0.0 954.8 %copy-start = (bf16[256,256]{1,0:T(8,128)(2,1)S(1)}, bf16[256,256]{1,0:T(8,128)(2,1)}, u32[]{:S(2)}) copy-start(bf16[256,256]{1,0:T(8,128)(2,1)} %param.23) | copy-start | bytes 393220
  1.7 63.4 %copy-start.4 = (s32[4096,2]{0,1:T(2,128)S(1)}, s32[4096,2]{0,1:T(2,128)}, u32[]{:S(2)}) copy-start(s32[4096,2]{0,1:T(2,128)} %param.17) | copy-start | bytes 98308
  53.1 87.4 %all-to-all-start.1 = ((s32[32,1,640]{2,1,0:T(1,128)}), s32[32,1,640]{2,1,0:T(1,128)S(1)}, u32[]{:S(2)}, u32[]{:S(2)}) async-start(s32[32,1,640]{2,1,0:T(1,128)} %bitcast.9), calls=%async_computation.1 | async-start | bytes 163840 | tf_op jit(solution)/shard_map/all_to_all | solution.py:62
  68.2 14.0 %copy-start.10 = (bf16[1024,32]{0,1:T(8,128)(2,1)S(1)}, bf16[1024,32]{0,1:T(8,128)(2,1)}, u32[]{:S(2)}) copy-start(bf16[1024,32]{0,1:T(8,128)(2,1)} %param.14) | copy-start | bytes 196612
  81.7 0.6 copy-start.1
  82.3 148.6 %copy-start.7 = (s32[8192,1]{0,1:T(1,128)}, s32[8192,1]{0,1:T(1,128)S(1)}, u32[]{:S(2)}) copy-start(s32[8192,1]{0,1:T(1,128)S(1)} %compare_select_fusion.4) | copy-start | bytes 98308
  140.5 100.2 %all-to-all-start = ((s32[32,1,512]{2,1,0:T(1,128)}), s32[32,1,512]{2,1,0:T(1,128)S(1)}, u32[]{:S(2)}, u32[]{:S(2)}) async-start(s32[32,1,512]{2,1,0:T(1,128)} %bitcast.3), calls=%async_computation | async-start | bytes 131072 | tf_op jit(solution)/shard_map/all_to_all | solution.py:75
  240.7 10.2 %copy-start.11 = (s32[1,1024]{1,0:T(1,128)S(1)}, s32[1,1024]{1,0:T(1,128)}, u32[]{:S(2)}) copy-start(s32[1,1024]{1,0:T(1,128)} %param.16) | copy-start | bytes 12292
  240.7 10.2 %copy-start.3 = (s32[1,1024,10]{1,0,2:T(1,128)S(1)}, s32[1,1024,10]{1,0,2:T(1,128)}, u32[]{:S(2)}) copy-start(s32[1,1024,10]{1,0,2:T(1,128)} %param.15) | copy-start | bytes 122884
  240.7 10.2 %copy-start.9 = (bf16[256,256]{1,0:T(8,128)(2,1)S(1)}, bf16[256,256]{1,0:T(8,128)(2,1)}, u32[]{:S(2)}) copy-start(bf16[256,256]{1,0:T(8,128)(2,1)} %param.18) | copy-start | bytes 393220
  240.7 242.7 %all-to-all-start.2 = ((bf16[32,640,256]{2,1,0:T(8,128)(2,1)}), bf16[32,640,256]{2,1,0:T(8,128)(2,1)}, u32[]{:S(2)}, u32[]{:S(2)}) async-start(bf16[32,640,256]{2,1,0:T(8,128)(2,1)} %broadcast_select_fusion), calls=%async_computation.2 | async-start | bytes 20971520 | tf_op jit(solution)/shard_map/all_to_all | solution.py:60
  483.4 139.3 %copy-start.6 = (bf16[256,256]{1,0:T(8,128)(2,1)S(1)}, bf16[256,256]{1,0:T(8,128)(2,1)}, u32[]{:S(2)}) copy-start(bf16[256,256]{1,0:T(8,128)(2,1)} %param.19) | copy-start | bytes 393220
  483.4 139.3 %copy-start.12 = (f32[256]{0:T(256)S(1)}, f32[256]{0:T(256)}, u32[]{:S(2)}) copy-start(f32[256]{0:T(256)} %param.20) | copy-start | bytes 3076
  696.3 19.9 %copy-start.2 = (s32[8192]{0:T(1024)S(1)}, s32[8192]{0:T(1024)}, u32[]{:S(2)}) copy-start(s32[8192]{0:T(1024)} %copy-done.1) | copy-start | bytes 98308
  696.3 22.7 %copy-start.8 = (s32[8192,1]{0,1:T(1,128)S(1)}, s32[8192,1]{0,1:T(1,128)}, u32[]{:S(2)}) copy-start(s32[8192,1]{0,1:T(1,128)} %copy-done.7) | copy-start | bytes 98308
  696.3 22.7 %copy-start.5 = (s32[4096,2]{0,1:T(2,128)S(1)}, s32[4096,2]{0,1:T(2,128)}, u32[]{:S(2)}) copy-start(s32[4096,2]{0,1:T(2,128)} %param.17) | copy-start | bytes 98308
  696.3 210.2 %all-to-all-start.3 = ((bf16[32,512,256]{2,1,0:T(8,128)(2,1)}), bf16[32,512,256]{2,1,0:T(8,128)(2,1)}, u32[]{:S(2)}, u32[]{:S(2)}) async-start(bf16[32,512,256]{2,1,0:T(8,128)(2,1)} %broadcast_select_fusion.1), calls=%async_computation.3 | async-start | bytes 16777216 | tf_op jit(solution)/shard_map/all_to_all | solution.py:72
  949.2 5.7 copy-start.14
  949.2 5.7 copy-start.15
  949.2 5.7 copy-start.16
  954.8 5.5 copy-start.13
where the time goes:
time: 977 us; the launch traced here: 967 us
  waiting for transfers between devices  419 us (43%)
  local copies, waits for them, and re-layouts  271 us (28%)
  matrix products  150 us (15%)
  starting transfers between devices  50.9 us (5%)
  other arithmetic  47.4 us (5%)
  blocking collectives  27 us (3%)
    all_to_all x1, waiting for transfers between devices, on_device(): lax.all_to_all(jnp.take(table, lax.all_to_all(requests, 'node', split_axi...  232 us
    all_to_all x1, waiting for transfers between devices, on_device(): lax.all_to_all(jnp.take(embed, lax.all_to_all(end_requests, 'node', split...  187 us
    dot_general x8, matrix products, one_block(): return jnp.dot(tallies, source, preferred_element_type=jnp.float32)  138 us
    gather x1, local copies, waits for them, and re-layouts, on_device(): jnp.take(table, lax.all_to_all(requests, 'node', split_axis=0, concat_axi...  80.8 us
    scatter x2, local copies, waits for them, and re-layouts, bucket(): requests = jnp.zeros((shards * capacity,), jnp.int32).at[target].set(offset)  69.6 us
    gather x1, local copies, waits for them, and re-layouts, on_device(): jnp.take(embed, lax.all_to_all(end_requests, 'node', split_axis=0, concat...  64.8 us
    gather x2, local copies, waits for them, and re-layouts, on_device(): ends = jnp.take(end_replies.reshape(-1, width), end_target, axis=0)  42.6 us
    all_gather x1, blocking collectives, on_device(): table = lax.all_gather(features, 'pair', axis=1, tiled=True)  27 us
  transfers between devices with their start and end apart: 4, of which 2 were waited for; matrix products, arithmetic and copies ran while one was open for 15% of the time, Pallas kernels for 0%

commit v1 on v0

v1 whole, which is shorter than its diff:
```python
import functools
import jax
import jax.numpy as jnp
from jax import lax
from jax.experimental import pallas as pl
from jax.experimental.pallas import tpu as pltpu
from jax.sharding import PartitionSpec as P

def gather_kernel(starts, keys, words, tab_hbm, wcat, bl, w1, b1, w2, b2, wo, out, tab, sums, selfs, sem, *, npair, span, U):
    cp = pltpu.make_async_copy(tab_hbm, tab, sem)
    cp.start(); cp.wait()
    mask16 = 65535

    def one(i, c):
        key = keys[i]
        e2 = (key & 8191) * 2
        n = lax.shift_right_logical(key, 13) & 32767
        base = n + lax.shift_right_logical(n, 10) * (4 * span)
        acc = None
        for j in range((c + 1) // 2):
            w = words[base + j * span]
            r = tab[w & mask16].astype(jnp.float32)
            acc = r if acc is None else acc + r
            if 2 * j + 1 < c:
                r = tab[lax.shift_right_logical(w, 16)].astype(jnp.float32)
                acc = acc + r
        if c > 1:
            acc = acc * jnp.float32(1.0 / c)
        return e2, n, acc

    def put(e2, n, acc):
        sums[pl.ds(e2, 2), :] = acc
        selfs[pl.ds(e2, 2), :] = tab[n].astype(jnp.float32)

    for c in range(1, 11):
        lo = starts[c - 1]
        hi = starts[c]
        nb = lax.div(hi - lo, U)
        def body(t, carry, c=c, lo=lo):
            res = [one(lo + t * U + u, c) for u in range(U)]
            for r in res: put(*r)
            return carry
        lax.fori_loop(0, nb, body, 0)
        def rem(t, carry, c=c):
            put(*one(t, c))
            return carry
        lax.fori_loop(lo + nb * U, hi, rem, 0)

    B = 512
    def dense(t, carry):
        embs = []
        for s in range(2):
            r0 = (s * npair + t * B) * 2
            xs = []
            for ref in (selfs, sums):
                for h in range(2):
                    xs.append(ref[pl.ds(r0 + h, B, 2), :].astype(jnp.bfloat16))
            x = jnp.concatenate(xs, axis=1)
            pre = jnp.dot(x, wcat[...], preferred_element_type=jnp.float32) + bl[...]
            r = jnp.maximum(pre, 0.0)
            ms = jnp.mean(r * r, axis=-1, keepdims=True)
            embs.append((r * lax.rsqrt(ms + 1e-6)).astype(jnp.bfloat16).astype(jnp.float32))
        had = (embs[0] * embs[1]).astype(jnp.bfloat16)
        first = jnp.maximum(jnp.dot(had, w1[...], preferred_element_type=jnp.float32) + b1[...], 0.0).astype(jnp.bfloat16)
        second = jnp.maximum(jnp.dot(first, w2[...], preferred_element_type=jnp.float32) + b2[...], 0.0)
        prod = second * wo[...]
        part = prod[:, :128] + prod[:, 128:]
        logit = lax.dot_general(jnp.ones((8, 128), jnp.float32), part, (((1,), (1,)), ((), ())), precision=lax.Precision.HIGHEST, preferred_element_type=jnp.float32)[:1]
        k = t * B + lax.broadcasted_iota(jnp.int32, (1, B), 1)
        z = jnp.where(k < npair // 4, -logit, logit)
        out[pl.ds(t, 1), :] = jnp.maximum(z, 0.0) + jnp.log1p(jnp.exp(-jnp.abs(z)))
        return carry
    lax.fori_loop(0, npair // B, dense, 0)

def score(starts, keys, words, table, wcat, bl, w1, b1, w2, b2, wo, U=5, npair=4096, span=1024):
    nodes = table.shape[0]
    smem = pl.BlockSpec(memory_space=pltpu.SMEM)
    vm = pl.BlockSpec(memory_space=pltpu.VMEM)
    return pl.pallas_call(
        functools.partial(gather_kernel, npair=npair, span=span, U=U),
        out_shape=jax.ShapeDtypeStruct((npair // 512, 512), jnp.float32),
        in_specs=[smem, smem, smem, pl.BlockSpec(memory_space=pl.ANY)] + [vm] * 7,
        out_specs=vm,
        scratch_shapes=[pltpu.VMEM((nodes, 2, 128), jnp.bfloat16), pltpu.VMEM((4 * npair, 128), jnp.float32), pltpu.VMEM((4 * npair, 128), jnp.float32), pltpu.SemaphoreType.DMA],
        compiler_params=pltpu.CompilerParams(vmem_limit_bytes=56 * 2**20),
    )(starts, keys, words, table, wcat, bl, w1, b1, w2, b2, wo)


def on_device(
    features, neighbors, counts, pairs, w_self, w_neigh, b_layer, w_one, b_one, w_two, b_two, w_out
):
    span, cols = features.shape
    shards = lax.axis_size("node")
    parts = lax.axis_size("pair")
    npair = pairs.shape[0]
    slab = lax.all_to_all(
        features.reshape(parts, span // parts, cols), "pair", split_axis=0, concat_axis=0, tiled=True
    )
    slab = slab.transpose(1, 0, 2).reshape(span // parts, 2, parts * cols // 2)
    table = lax.all_gather(slab, ("node", "pair"), axis=0, tiled=True)
    ids = neighbors[0].T
    words = ids[0::2] | (ids[1::2] << 16)
    info = lax.all_gather(jnp.concatenate([words, counts], axis=0), "node", axis=0)
    words = info[:, :5].reshape(-1)
    ends = pairs.T.reshape(-1)
    cnt = jnp.take(info[:, 5].reshape(-1), ends, axis=0)
    key = ((cnt - 6) << 28) | (ends << 13) | jnp.arange(2 * npair, dtype=jnp.int32)
    key = lax.sort(key)
    starts = jnp.sum(
        (cnt[None, :] <= jnp.arange(11, dtype=jnp.int32)[:, None]).astype(jnp.int32), axis=1
    )
    row = lambda v: v.reshape(1, -1)
    loss = score(
        starts, key, words, table, jnp.concatenate([w_self, w_neigh], axis=0), row(b_layer),
        w_one, row(b_one), w_two, row(b_two), row(w_out), npair=npair, span=span,
    )
    return loss.reshape(-1)


def solution(mesh):
    in_specs = (
        P("node", "pair"),
        P("pair", "node", None),
        P("pair", "node"),
        P(("pair", "node"), None),
    ) + (P(),) * 8
    return jax.shard_map(
        on_device, mesh=mesh, in_specs=in_specs, out_specs=P(("pair", "node")), check_vma=False
    )
```

time: 977 us -> 259 us (0.27)
  waiting for transfers between devices: 419 us -> 25.2 us
  local copies, waits for them, and re-layouts: 271 us -> 52 us
  matrix products: 150 us -> 0 us
  Pallas kernels: 0 us -> 104 us
  starting transfers between devices: 50.9 us -> 0.01 us
  other arithmetic: 47.4 us -> 8.96 us
  blocking collectives: 27 us -> 54 us
  between operations: 0.84 us -> 13.5 us
    all_to_all x4 -> x0, waiting for transfers between devices: 419 us -> none  [the longest x1 232 us: on_device(): lax.all_to_all(jnp.take(table, lax.all_to_all(requests, 'node', split_axi...]
    dot_general x12 -> x0, matrix products: 150 us -> none  [the longest x8 138 us: one_block(): return jnp.dot(tallies, source, preferred_element_type=jnp.float32)]
    gather x4 -> x1, local copies, waits for them, and re-layouts: 188 us -> 45.5 us  [on_device(): cnt = jnp.take(info[:, 5].reshape(-1), ends, axis=0)]
    pallas_call x0 -> x1, Pallas kernels: none -> 104 us  [score(): pl.pallas_call(functools.partial(gather_kernel, npair=npair, span=span, U...]
    scatter x2 -> x0, local copies, waits for them, and re-layouts: 69.6 us -> none  [bucket(): requests = jnp.zeros((shards * capacity,), jnp.int32).at[target].set(offset)]
    all_to_all x4 -> x0, starting transfers between devices: 50.9 us -> none  [the longest x1 19.9 us: on_device(): lax.all_to_all(jnp.take(embed, lax.all_to_all(end_requests, 'node', split...]
    all_gather x0 -> x1, waiting for transfers between devices: none -> 25.2 us  [on_device(): table = lax.all_gather(slab, ('node', 'pair'), axis=0, tiled=True)]
    select_n x11 -> x1, other arithmetic: 24.7 us -> 0.04 us  [on_device(): cnt = jnp.take(info[:, 5].reshape(-1), ends, axis=0)]
  transfers between devices with their start and end apart: 4 -> 1, of which waited for: 2 -> 1; matrix products, arithmetic and copies ran while one was open for 15% -> 22% of each run, Pallas kernels for 0% -> 0%
where the time goes in v1:
time: 259 us; the launch traced here: 258 us
  Pallas kernels  104 us (40%)
  blocking collectives  54 us (21%)
  local copies, waits for them, and re-layouts  52 us (20%)
  waiting for transfers between devices  25.2 us (10%)
  between operations  13.5 us (5%)
  other arithmetic  8.96 us (3%)
    pallas_call x1, Pallas kernels, score(): pl.pallas_call(functools.partial(gather_kernel, npair=npair, span=span, U...  104 us
    gather x1, local copies, waits for them, and re-layouts, on_device(): cnt = jnp.take(info[:, 5].reshape(-1), ends, axis=0)  45.5 us
    all_gather x1, blocking collectives, on_device(): lax.all_gather(jnp.concatenate([words, counts], axis=0), 'node', axis=0)  43.6 us
    all_gather x1, waiting for transfers between devices, on_device(): table = lax.all_gather(slab, ('node', 'pair'), axis=0, tiled=True)  25.2 us
    all_to_all x1, blocking collectives, on_device(): lax.all_to_all(features.reshape(parts, span // parts, cols), 'pair', spli...  10.5 us
    sort x1, other arithmetic, on_device(): key = lax.sort(key)  6.79 us
  transfers between devices with their start and end apart: 1, of which 1 were waited for; matrix products, arithmetic and copies ran while one was open for 22% of the time, Pallas kernels for 0%

profile of v1, /device:TPU:1, one launch (start us, length us, event | category | flops | bytes accessed | tf_op | source)
XLA Modules:
  0.0 258.1 jit_solution(17591815047747306456)
XLA Ops:
  6.5 0.0 copy-start
  6.5 0.0 all-gather.4.cloned.1.call-start
  6.5 0.8 copy-done
  7.4 10.5 %all_to_all.5 = bf16[8,128,32]{1,2,0:T(8,128)(2,1)S(1)} all-to-all(bf16[8,128,32]{1,2,0:T(8,128)(2,1)S(1)} %copy_bitcast_fusion), channel_id=1, replica_groups=mesh['pair'=8,'node'=32] {'pair'}, dimensions={0} | all-to-all | bytes 131072 | tf_op jit(solution)/shard_map/all_to_all | solution.py:96
  17.9 0.7 copy.20
  18.6 0.0 all-gather.4.cloned.1.call-update
  18.6 0.8 copy.28
  19.5 0.8 copy.23
  20.2 0.7 add_bitcast_fusion
  20.9 43.6 %all-gather.1 = s32[32,6,1024]{2,1,0:T(8,128)S(1)} all-gather(s32[1,6,1024]{2,1,0:T(8,128)S(1)} %add_bitcast_fusion), channel_id=2, replica_groups=mesh['pair'=8,'node'=32] {'node'}, dimensions={0}, use_global_device_ids=true | all-gather | bytes 811008 | tf_op jit(solution)/shard_map/all_gather | solution.py:103
  64.5 0.1 slice.18
  64.6 0.8 copy.24
  65.4 1.0 reshape.84.words
  66.5 0.0 copy-start.1
  66.5 0.0 copy-start.2
  66.5 45.5 %gather_fusion = s32[8192]{0:T(1024)S(1)} fusion(s32[32768]{0:T(1024)S(1)} %bitcast.31, s32[8192]{0:T(1024)S(1)} %broadcast_clamp_fusion), kind=kCustom, calls=%fused_computation | custom fusion | bytes 98304 | tf_op jit(solution)/shard_map/jit(_take)/gather | solution.py:106
  112.1 6.8 %sort.10 = (s32[8192]{0:T(1024)}, s32[8192]{0:T(1024)}) sort(s32[8192]{0:T(1024)S(1)} %get-tuple-element.8, s32[8192]{0:T(1024)S(1)} %iota.11), dimensions={0}, to_apply=%region_1.2 | sort | flops 106496 | bytes 131072 | tf_op jit(solution)/shard_map/sort | solution.py:108
  118.9 0.0 copy-done.1
  118.9 0.0 copy-done.2
  118.9 0.7 pad_maximum_fusion.wcat
  119.6 0.7 convert_reduce_fusion.starts
  120.3 25.2 %all-gather.4.cloned.1.call-done.tab_hbm = bf16[32768,2,128]{2,1,0:T(2,128)(2,1)} async-done(((bf16[128,2,128]{2,1,0:T(2,128)(2,1)}), bf16[32768,2,128]{2,1,0:T(2,128)(2,1)}) %all-gather.4.cloned.1.call-update) | async-done | bytes 16777232 | tf_op jit(solution)/shard_map/all_gather | solution.py:100
  145.5 104.5 %shard_map.118 = f32[8,512]{1,0:T(8,128)} custom-call(s32[11]{0:T(128)} %convert_reduce_fusion.starts, s32[8192]{0:T(1024)} %get-tuple-element.7.keys, s32[163840]{0:T(1024)} %reshape.84.words, bf16[32768,2,128]{2,1,0:T(2,128)(2,1)} %all-gather.4.cloned.1.call-done.tab_hbm, bf16[512,256]{1,0:T(8,128)(2,1)} %pad_maximum_fusion.wcat, f32[1,256]{1,0:T(1,128)} %bitcast.42, ...), custom_call_target="tpu_custom_call" | custom-call | tf_op jit(solution)/shard_map/pallas_call | solution.py:79
  250.0 1.3 copy.25
  (8 shorter events, 0.1 us)
Async XLA Ops:
  6.5 0.8 copy-start
  6.5 139.0 %all-gather.4.cloned.1.call-start = ((), (), s32[]{:S(2)}) async-start(), calls=%async_computation.1 | async-start | bytes 16842752 | tf_op jit(solution)/shard_map/all_gather | solution.py:100
  66.5 52.4 %copy-start.1 = (bf16[256,256]{1,0:T(8,128)(2,1)S(1)}, bf16[256,256]{1,0:T(8,128)(2,1)}, u32[]{:S(2)}) copy-start(bf16[256,256]{1,0:T(8,128)(2,1)} %param.17) | copy-start | bytes 393220
  66.5 52.4 %copy-start.2 = (bf16[256,256]{1,0:T(8,128)(2,1)S(1)}, bf16[256,256]{1,0:T(8,128)(2,1)}, u32[]{:S(2)}) copy-start(bf16[256,256]{1,0:T(8,128)(2,1)} %param.16) | copy-start | bytes 393220
Sparse Core Ops, SparseCore 0:
  18.7 126.7 all-gather.3
